TPU v7x, 256 devices: a whole 4x4x8 slice. The times are simulated.
256 devices in a mesh: horiz: 16 (over z, core), lev: 4 (over y), fld: 4 (over x).
Axes of the slice: x: 4, y: 4, z: 8, core: 2. Of those that a mesh axis runs over, the one named last changes fastest.
Arguments:
- adj_out: bfloat16 [8, 64, 2048, 128], P('fld', 'lev', 'horiz'), may hold values from -6 to 6
- interp: bfloat16 [2048, 128, 128], P('horiz'), may hold values from -0.5 to 0.5
- vert_wts: float32 [64, 4], P('lev'), may hold values from -3 to 3
- vert_base: int32 [64], P('lev'), may hold values from -1 to 63, as said below
- dep_tile: int32 [2048], P('horiz'), may hold values from 0 to 2047, as said below
- traj_grad: bfloat16 [2, 8, 64, 2048, 128], P(None, 'fld', 'lev', 'horiz'), may hold values from -0.25 to 0.25
Outputs:
- adj_field: float32 [8, 64, 2048, 128], P('fld', 'lev', 'horiz')
- adj_disp: float32 [2, 2048, 128], P(None, 'horiz')
Inputs may be any that keep to these rules, and one draw needn't show every extreme that they name: vert_base[l] is l or l - 1; vert_base[0] is -1 and vert_base[63] is 63. `dep_tile`: tiles form blocks of 128 in order, numbered cyclically. The departure tile (the tile's stencils written as one dense matrix, shared by all levels) of an arrival tile lies in the arrival tile's own block, the next block, the previous one, or the block half the number of blocks away (across the pole). Of one block's arrival tiles at most 32 depart from each of these other blocks (with two blocks: at most 32 from the other block); some block reaches 32 from the next block, some block receives 32 from the previous one, and some block reaches 32 from the block across the pole.
All inputs are finite; a program needn't handle non-finite values.
Results may differ from a plain program's by a relative error of at most 0.0003.
Values sent between devices are 32-bit elements; how exact they have to be, the bound alone decides.
A program may use at most 128 MiB of HBM per device.

v0:
```python
import jax
import jax.numpy as jnp
from jax import lax
from jax.sharding import PartitionSpec as P

CAP = 32


def shifted(block, axis, distance):
    devices = range(lax.axis_size(axis))
    route = [(i - distance, i) for i in devices if i - distance in devices]
    return lax.ppermute(block, axis, route)


def vertical_matrix(vert_wts, vert_base, first, extent):
    levels = first - 2 + jnp.arange(extent, dtype=jnp.int32)
    taps = vert_base[:, None] - 1 + jnp.arange(4, dtype=jnp.int32)[None, :]
    hits = (levels[:, None, None] == taps[None, :, :]).astype(jnp.float32)
    return jnp.sum(hits * vert_wts[None, :, :], axis=2)


def pack_slots(group, groups, local_id, horiz, slots):
    tiles = horiz.shape[2]
    members = jnp.arange(groups, dtype=jnp.int32)
    inside = group[None, :] == members[:, None]
    rank = (
        jnp.sum(jnp.cumsum(inside.astype(jnp.int32), axis=1) * inside.astype(jnp.int32), axis=0) - 1
    )
    slot = jnp.where(group >= 0, group * slots + rank, groups * slots)
    source = jnp.full((groups * slots,), tiles, jnp.int32)
    source = source.at[slot].set(jnp.arange(tiles, dtype=jnp.int32), mode="drop")
    packed = jnp.take(horiz, source, axis=2, mode="fill", fill_value=0.0)
    target = jnp.take(local_id, source, mode="fill", fill_value=0)
    labels = jnp.where(source < tiles, target, -1).astype(jnp.float32)
    return (packed, labels.reshape(1, 1, -1, 1))


def take_in(total, packed, labels):
    tiles = total.shape[2]
    ident = labels.reshape(-1).astype(jnp.int32)
    ident = jnp.where(ident < 0, tiles, ident)
    padded = jnp.zeros(total.shape[:2] + (tiles + 1,) + total.shape[3:], jnp.float32)
    padded = padded.at[:, :, ident, :].add(packed)
    return total + padded[:, :, :tiles]


def shards(adj_out, interp, vert_wts, vert_base, dep_tile, traj_grad):
    nlev = adj_out.shape[1]
    tiles = adj_out.shape[2]
    blocks = lax.axis_size("horiz")
    here = lax.axis_index("horiz")
    horiz = jnp.einsum("fltp,tpq->fltq", adj_out, interp, preferred_element_type=jnp.float32)
    owner = dep_tile // tiles
    local_id = dep_tile - owner * tiles
    offset = jnp.remainder(owner - here, blocks)
    stay = offset == 0
    own_ids = jnp.where(stay, local_id, tiles)
    total = jnp.zeros(horiz.shape[:2] + (tiles + 1,) + horiz.shape[3:], jnp.float32)
    total = total.at[:, :, own_ids, :].add(horiz)[:, :, :tiles]
    group = jnp.where(stay, -1, owner)
    packed, labels = pack_slots(group, blocks, local_id, horiz, CAP)
    arrived, arrived_labels = (
        lax.all_to_all(packed, "horiz", split_axis=2, concat_axis=2, tiled=True),
        lax.all_to_all(labels, "horiz", split_axis=2, concat_axis=2, tiled=True),
    )
    total = take_in(total, arrived, arrived_labels)
    first = lax.axis_index("lev") * nlev
    vertical = vertical_matrix(vert_wts, vert_base, first, nlev + 4)
    spread = jnp.einsum("el,fltq->fetq", vertical, total, precision=lax.Precision.HIGHEST)
    from_below = shifted(spread[:, nlev + 2 :], "lev", 1)
    from_above = shifted(spread[:, :2], "lev", -1)
    adj_field = spread[:, 2 : nlev + 2]
    adj_field = adj_field.at[:, :2].add(from_below)
    adj_field = adj_field.at[:, nlev - 2 :].add(from_above)
    partial_disp = jnp.einsum(
        "fltp,cfltp->ctp", adj_out, traj_grad, preferred_element_type=jnp.float32
    )
    adj_disp = lax.psum(partial_disp, ("lev", "fld"))
    return (adj_field, adj_disp)


def solution(mesh):
    return jax.shard_map(
        shards,
        mesh=mesh,
        in_specs=(
            P("fld", "lev", "horiz", None),
            P("horiz", None, None),
            P("lev", None),
            P("lev"),
            P("horiz"),
            P(None, "fld", "lev", "horiz", None),
        ),
        out_specs=(P("fld", "lev", "horiz", None), P(None, "horiz", None)),
        check_vma=False,
    )
```

profile of v0, /device:TPU:1, one launch (start us, length us, event | category | flops | bytes accessed | tf_op | source)
XLA Modules:
  0.0 415.0 jit_solution(6794098694644747419)
XLA Ops:
  7.2 0.0 copy-start.4
  7.2 0.8 compare_select_fusion.4
  8.0 0.3 reduce_window_sum.11
  8.3 1.0 scatter_custom_fusion.1
  9.3 3.3 gather_fusion
  12.7 0.9 copy.23
  13.5 10.0 %all-to-all-start = ((f32[1,1,512,1]{3,1,0,2:T(1,128)}), f32[1,1,512,1]{3,1,0,2:T(1,128)S(1)}, u32[]{:S(2)}, u32[]{:S(2)}) async-start(f32[1,1,512,1]{3,1,0,2:T(1,128)} %copy.23), calls=%async_computation | async-start | bytes 524288 | tf_op jit(solution)/shard_map/all_to_all | solution.py:64
  23.5 0.0 copy-done.4
  23.5 0.7 copy.22
  24.2 3.4 fusion.11
  27.6 4.4 %gather_fusion.1 = f32[512,2,16,128]{3,2,1,0:T(8,128)} fusion(f32[2,16,128,128]{3,1,0,2:T(8,128)S(1)} %bitcast.28, s32[1024]{0:T(1024)S(1)} %pad_clamp_fusion), kind=kCustom, calls=%fused_computation.1 | custom fusion | bytes 16779264 | tf_op jit(solution)/shard_map/jit(_take)/gather | solution.py:32
  32.0 6.3 %select_bitcast_fusion = f32[2,16,512,128]{3,1,0,2:T(8,128)} fusion(f32[512,2,16,128]{3,2,1,0:T(8,128)} %gather_fusion.1, pred[512]{0:T(512)(128)(4,1)S(1)} %compare_and_fusion), kind=kLoop, calls=%fused_computation.5 | loop fusion | flops 2097152 | bytes 16777728 | tf_op jit(solution)/shard_map/jit(_take)/select_n | solution.py:32
  38.2 0.0 all-to-all-done
  38.2 7.2 %all-to-all-start.1 = ((f32[2,16,512,128]{3,1,0,2:T(8,128)}), f32[2,16,512,128]{3,1,0,2:T(8,128)}, u32[]{:S(2)}, u32[]{:S(2)}) async-start(f32[2,16,512,128]{3,1,0,2:T(8,128)} %select_bitcast_fusion), calls=%async_computation.1 | async-start | bytes 16777216 | tf_op jit(solution)/shard_map/all_to_all | solution.py:63
  45.5 0.2 all-reduce.2.cloned.1.call-start
  45.7 1.5 broadcast.125.clone.1
  47.2 0.0 copy-start.8
  47.2 16.7 %scatter_fusion = f32[2,16,129,128]{3,1,2,0:T(8,128)} fusion(f32[2,16,129,128]{3,1,2,0:T(8,128)} %broadcast.125.clone.1, s32[128]{0:T(128)S(1)} %get-tuple-element.36, f32[128,2,16,128]{3,2,1,0:T(8,128)S(1)} %bitcast.29), kind=kCustom, calls=%fused_computation.2 | custom fusion | flops 524288 | bytes 6291968 | tf_op jit(solution)/shard_map/scatter-add | solution.py:59
  63.9 0.0 copy-done.8
  63.9 0.0 copy-done.7
  63.9 0.1 select_reduce_fusion
  64.0 1.6 bitcast_convert_fusion
  65.6 9.1 %convert_reduce_fusion = s32[512]{0:T(512)S(1)} fusion(f32[1,1,512,1]{3,1,0,2:T(1,128)S(1)} %all-to-all-done), kind=kLoop, calls=%fused_computation.16 | loop fusion | flops 512 | bytes 4096 | tf_op jit(solution)/shard_map/convert_element_type | solution.py:40
  74.7 154.3 %all-to-all-done.1 = f32[2,16,512,128]{3,1,0,2:T(8,128)} async-done(((f32[2,16,512,128]{3,1,0,2:T(8,128)}), f32[2,16,512,128]{3,1,0,2:T(8,128)}, u32[]{:S(2)}, u32[]{:S(2)}) %all-to-all-start.1) | async-done | bytes 8388640 | tf_op jit(solution)/shard_map/all_to_all | solution.py:63
  229.0 1.5 broadcast.125.clone
  230.5 74.1 %scatter_fusion.1 = f32[2,16,129,128]{3,1,2,0:T(8,128)} fusion(f32[2,16,129,128]{3,1,2,0:T(8,128)} %broadcast.125.clone, s32[512]{0:T(512)S(1)} %bitcast.33, f32[512,2,16,128]{3,2,1,0:T(8,128)} %bitcast.10), kind=kCustom, calls=%fused_computation.4 | custom fusion | flops 2097152 | bytes 25167872 | tf_op jit(solution)/shard_map/scatter-add | solution.py:43
  304.6 0.0 copy-done
  304.6 4.5 %fusion.2 = f32[2,20,128,128]{3,1,2,0:T(8,128)S(1)} fusion(f32[2,16,129,128]{3,1,2,0:T(8,128)} %scatter_fusion.1, f32[2,16,129,128]{3,1,2,0:T(8,128)S(1)} %copy-done, f32[20,16]{0,1:T(8,128)S(1)} %select_reduce_fusion), kind=kOutput, calls=%fused_computation.10 | convolution fusion | flops 126353408 | bytes 6823936 | tf_op jit(solution)/shard_map/el,fltq->fetq/dot_general | solution.py:69
  309.1 0.0 copy-start.1
  309.2 1.7 copy-done.1
  310.8 1.0 fusion.10
  311.8 3.5 collective-permute-start
  315.3 0.0 copy-done.3
  315.3 0.0 copy-done.5
  315.3 1.1 multiply_reduce_fusion
  316.4 0.0 all-reduce.2.cloned.1.call-update
  316.4 0.0 copy-done.2
  316.5 0.0 copy-start.6
  316.5 0.2 slice.87
  316.7 0.7 copy-done.6
  317.4 1.3 collective-permute-start.1
  318.7 1.6 collective-permute-done
  320.3 0.2 fusion.4
  320.6 5.4 %collective-permute-done.1 = f32[2,2,128,128]{3,1,2,0:T(2,128)S(1)} collective-permute-done((f32[2,2,128,128]{3,1,2,0:T(2,128)S(1)}, f32[2,2,128,128]{3,1,2,0:T(2,128)S(1)}, u32[]{:S(2)}, u32[]{:S(2)}) %collective-permute-start.1) | collective-permute-done | bytes 262176 | tf_op jit(solution)/shard_map/ppermute | solution.py:12
  326.0 0.3 fusion.3
  326.2 1.9 copy.24
  328.2 78.4 %all-reduce.2.cloned.1.call-done = f32[2,128,128]{2,1,0:T(8,128)} async-done(((f32[2,128,128]{2,1,0:T(8,128)}), f32[2,128,128]{2,1,0:T(8,128)}) %all-reduce.2.cloned.1.call-update) | async-done | bytes 131088 | tf_op jit(solution)/shard_map/psum | solution.py:78
  406.6 1.6 copy.39
  (18 shorter events, 0.1 us)
Async XLA Ops:
  7.2 16.4 %copy-start.4 = (bf16[2,16,128,128]{3,2,1,0:T(8,128)(2,1)S(1)}, bf16[2,16,128,128]{3,2,1,0:T(8,128)(2,1)}, u32[]{:S(2)}) copy-start(bf16[2,16,128,128]{3,2,1,0:T(8,128)(2,1)} %param.10) | copy-start | bytes 3145732
  13.5 24.7 %all-to-all-start = ((f32[1,1,512,1]{3,1,0,2:T(1,128)}), f32[1,1,512,1]{3,1,0,2:T(1,128)S(1)}, u32[]{:S(2)}, u32[]{:S(2)}) async-start(f32[1,1,512,1]{3,1,0,2:T(1,128)} %copy.23), calls=%async_computation | async-start | bytes 524288 | tf_op jit(solution)/shard_map/all_to_all | solution.py:64
  38.2 190.8 %all-to-all-start.1 = ((f32[2,16,512,128]{3,1,0,2:T(8,128)}), f32[2,16,512,128]{3,1,0,2:T(8,128)}, u32[]{:S(2)}, u32[]{:S(2)}) async-start(f32[2,16,512,128]{3,1,0,2:T(8,128)} %select_bitcast_fusion), calls=%async_computation.1 | async-start | bytes 16777216 | tf_op jit(solution)/shard_map/all_to_all | solution.py:63
  45.5 361.1 %all-reduce.2.cloned.1.call-start = ((), (), s32[]{:S(2)}) async-start(), calls=%async_computation.2 | async-start | bytes 262144 | tf_op jit(solution)/shard_map/psum | solution.py:78
  47.2 16.7 %copy-start.8 = (s32[16]{0:T(128)S(1)}, s32[16]{0:T(128)}, u32[]{:S(2)}) copy-start(s32[16]{0:T(128)} %param.13) | copy-start | bytes 196
  47.2 16.7 %copy-start.7 = (f32[16,4]{0,1:T(4,128)S(1)}, f32[16,4]{0,1:T(4,128)}, u32[]{:S(2)}) copy-start(f32[16,4]{0,1:T(4,128)} %param.12) | copy-start | bytes 772
  230.5 74.1 %copy-start = (f32[2,16,129,128]{3,1,2,0:T(8,128)S(1)}, f32[2,16,129,128]{3,1,2,0:T(8,128)}, u32[]{:S(2)}) copy-start(f32[2,16,129,128]{3,1,2,0:T(8,128)} %scatter_fusion) | copy-start | bytes 6340612
  304.6 10.6 %copy-start.3 = (f32[128,128,2,16]{1,0,3,2:T(8,128)S(1)}, f32[128,128,2,16]{1,0,3,2:T(8,128)}, u32[]{:S(2)}) copy-start(f32[128,128,2,16]{1,0,3,2:T(8,128)} %bitcast_convert_fusion) | copy-start | bytes 6291460
  304.6 10.6 %copy-start.5 = (bf16[2,2,16,128,128]{4,3,2,1,0:T(8,128)(2,1)S(1)}, bf16[2,2,16,128,128]{4,3,2,1,0:T(8,128)(2,1)}, u32[]{:S(2)}) copy-start(bf16[2,2,16,128,128]{4,3,2,1,0:T(8,128)(2,1)} %param.15) | copy-start | bytes 6291460
  309.1 1.7 copy-start.1
  311.8 4.7 %copy-start.2 = (f32[2,20,128,128]{3,1,2,0:T(8,128)S(1)}, f32[2,20,128,128]{3,1,2,0:T(8,128)}, u32[]{:S(2)}) copy-start(f32[2,20,128,128]{3,1,2,0:T(8,128)} %copy-done.1) | copy-start | bytes 7864324
  311.8 8.5 %collective-permute-start = (f32[2,2,128,128]{3,1,2,0:T(2,128)}, f32[2,2,128,128]{3,1,2,0:T(2,128)S(1)}, u32[]{:S(2)}, u32[]{:S(2)}) collective-permute-start(f32[2,2,128,128]{3,1,2,0:T(2,128)} %get-tuple-element.41), channel_id=1, source_target_pairs={{0,4},{4,8},{8,12},{1,5},{5,9},{9,13},{2,6},{6,10},{10,14},{3,7},{... | collective-permute-start | bytes 786440 | tf_op jit(solution)/shard_map/ppermute | solution.py:12
  316.5 1.0 copy-start.6
  317.4 8.5 %collective-permute-start.1 = (f32[2,2,128,128]{3,1,2,0:T(2,128)S(1)}, f32[2,2,128,128]{3,1,2,0:T(2,128)S(1)}, u32[]{:S(2)}, u32[]{:S(2)}) collective-permute-start(f32[2,2,128,128]{3,1,2,0:T(2,128)S(1)} %copy-done.6), channel_id=1, source_target_pairs={{4,0},{8,4},{12,8},{5,1},{9,5},{13,9},{6,2},{10,6},{14,10},{7,3},{... | collective-permute-start | bytes 786440 | tf_op jit(solution)/shard_map/ppermute | solution.py:12
Sparse Core Ops, SparseCore 0:
  316.6 89.9 all-reduce.1
where the time goes:
time: 417 us; the launch traced here: 415 us
  waiting for transfers between devices  240 us (58%)
  other arithmetic  111 us (27%)
  starting transfers between devices  22.2 us (5%)
  local copies, waits for them, and re-layouts  20.4 us (5%)
  between operations  14.2 us (3%)
  matrix products  7.9 us (2%)
    all_to_all x1, waiting for transfers between devices, shards(): lax.all_to_all(packed, 'horiz', split_axis=2, concat_axis=2, tiled=True)  154 us
    psum x1, waiting for transfers between devices, shards(): adj_disp = lax.psum(partial_disp, ('lev', 'fld'))  78.4 us
    scatter-add x1, other arithmetic, take_in(): padded = padded.at[:, :, ident, :].add(packed)  74.1 us
    scatter-add x1, other arithmetic, shards(): total = total.at[:, :, own_ids, :].add(horiz)[:, :, :tiles]  16.7 us
    all_to_all x1, starting transfers between devices, shards(): lax.all_to_all(labels, 'horiz', split_axis=2, concat_axis=2, tiled=True)  9.98 us
    convert_element_type x1, other arithmetic, take_in(): ident = labels.reshape(-1).astype(jnp.int32)  9.13 us
  transfers between devices with their start and end apart: 5, of which 4 were waited for; matrix products, arithmetic and copies ran while one was open for 11% of the time, Pallas kernels for 0%

commit v1 on v0

v1 whole, which is shorter than its diff:
```python
import functools

import jax
import jax.numpy as jnp
from jax import lax
from jax.experimental import pallas as pl
from jax.experimental.pallas import tpu as pltpu
from jax.sharding import PartitionSpec as P

MESH = pl.DeviceIdType.MESH
CAP = 32
ROLES = 3
GROUP = 8
GROUPS = CAP // GROUP
SLOTS = ROLES * CAP
F32, BF16 = jnp.float32, jnp.bfloat16


def split(values):
    high = values.astype(BF16)
    low = (values - high.astype(F32)).astype(BF16)
    return jnp.concatenate([high, low], axis=1)


def spread(hit, values):
    both = jnp.dot(hit, split(values), preferred_element_type=F32)
    width = values.shape[1]
    return both[:, :width] + both[:, width:]


def kernel(
    blocks, levs, flds, nf, nl, tiles,
    adj_hbm, interp_hbm, traj_hbm, dep_ref, wts_ref, base_ref,
    out_hbm, disp_ref,
    adj, interp, traj, adj32, h_slot, h_own, snd, rcv,
    slot_dn, slot_up, slot_dn_in, slot_up_in, own_dn, own_up, own_dn_in, own_up_in,
    acc, label, label_in, index_v, index_s, part, part_x, part_y, whole,
    in_sem, index_sem, out_sem, z_send, z_recv, halo_send, halo_recv, disp_send, disp_recv,
):
    fl = nf * nl
    here, lev, fld = lax.axis_index("horiz"), lax.axis_index("lev"), lax.axis_index("fld")
    core = lax.rem(here, 2)
    pole = lax.rem(here + blocks // 2, blocks)
    across = lax.rem(here + 2 * core - 1 + blocks, blocks)
    mate = here + 1 - 2 * core
    up, down = lax.rem(lev + 1, levs), lax.rem(lev + levs - 1, levs)

    loads = [
        pltpu.make_async_copy(adj_hbm, adj, in_sem.at[0]),
        pltpu.make_async_copy(interp_hbm, interp, in_sem.at[1]),
        pltpu.make_async_copy(traj_hbm, traj, in_sem.at[2]),
    ]
    for load in loads:
        load.start()

    barrier = pltpu.get_barrier_semaphore()
    peers = [{"horiz": pole}, {"horiz": across}, {"horiz": mate}]
    peers += [{"lev": lax.rem(lev + d, levs)} for d in range(1, levs)]
    peers += [{"fld": lax.rem(fld + d, flds)} for d in range(1, flds)]
    for peer in peers:
        pl.semaphore_signal(barrier, inc=1, device_id=peer, device_id_type=MESH)

    square = (tiles, tiles)
    by_lane = jnp.broadcast_to(dep_ref[...], square)
    by_row = by_lane.T
    lane = lax.broadcasted_iota(jnp.int32, square, 1)
    row = lax.broadcasted_iota(jnp.int32, square, 0)

    def role_of(dep):
        owner = dep // tiles
        return jnp.where(owner == pole, 0, jnp.where(owner == across, 1, jnp.where(owner == mate, 2, ROLES)))

    lane_role, row_role = role_of(by_lane), role_of(by_row)
    before = jnp.where((lane_role == row_role) & (row < lane), 1, 0)
    rank = jnp.sum(before, axis=0, keepdims=True)
    slot = jnp.where(lane_role < ROLES, lane_role * CAP + rank, -1)
    chosen = slot.T == lane
    source = jnp.sum(jnp.where(chosen, row, 0), axis=0, keepdims=True)
    target = jnp.sum(jnp.where(chosen, lax.rem(by_row, tiles) + 1, 0), axis=0, keepdims=True) - 1
    index_v[...] = jnp.broadcast_to(source, index_v.shape)
    label[...] = jnp.broadcast_to(target, label.shape)
    index_copy = pltpu.make_async_copy(index_v, index_s, index_sem)
    index_copy.start()
    own_hit = jnp.where((lane_role == ROLES) & (lax.rem(by_lane, tiles) == row), 1.0, 0.0).astype(BF16)

    first = lev * nl
    coef = []
    for l in range(nl):
        late = base_ref[l] < first + l
        taps = [wts_ref[l, j] for j in range(4)]
        coef.append([
            jnp.where(late, taps[k] if k < 4 else 0.0, taps[k - 1] if k > 0 else 0.0) for k in range(5)
        ])

    def vertical(values, emit):
        for e in range(nl + 4):
            total = None
            for l in range(max(0, e - 4), min(nl - 1, e) + 1):
                term = coef[l][e - l] * values[l]
                total = term if total is None else total + term
            emit(e, total)

    loads[0].wait()

    def widen(i, carry):
        adj32[pl.ds(pl.multiple_of(i * tiles, tiles), tiles), :] = adj[i].astype(F32)
        return carry

    lax.fori_loop(0, fl, widen, 0)
    index_copy.wait()
    loads[1].wait()

    def horizontal(t, s, dest, extent):
        rows = [adj32[pl.ds(t + b * 8 * tiles, 8, stride=tiles), :] for b in range(fl // 8)]
        value = jnp.dot(jnp.concatenate(rows, axis=0).astype(BF16), interp[t], preferred_element_type=F32)
        for b in range(fl // 8):
            dest[pl.ds(s + b * 8 * extent, 8, stride=extent), :] = value[b * 8 : b * 8 + 8]

    def work(g):
        at = pl.multiple_of(g * GROUP, GROUP)
        for i in range(GROUP):
            horizontal(index_s[0, at + i], at + i, h_slot, SLOTS)
        for f in range(nf):
            values = [
                h_slot[pl.ds(pl.multiple_of((f * nl + l) * SLOTS + at, GROUP), GROUP), :] for l in range(nl)
            ]

            def emit(e, value, f=f):
                if e < 2:
                    slot_dn[f, e, pl.ds(at, GROUP), :] = value
                elif e < nl + 2:
                    snd[f, e - 2, pl.ds(at, GROUP), :] = value
                else:
                    slot_up[f, e - nl - 2, pl.ds(at, GROUP), :] = value

            vertical(values, emit)

    def inner(g):
        role = g // GROUPS
        partner = jnp.where(role == 0, pole, jnp.where(role == 1, across, mate))
        at = pl.multiple_of(g * GROUP, GROUP)
        piece = (slice(None), pl.ds(2, nl - 4), pl.ds(at, GROUP), slice(None))
        return pltpu.make_async_remote_copy(
            src_ref=snd.at[piece], dst_ref=rcv.at[piece],
            send_sem=z_send.at[g], recv_sem=z_recv.at[g],
            device_id={"horiz": partner}, device_id_type=MESH,
        )

    work(0)
    pl.semaphore_wait(barrier, len(peers))
    inner(0).start()

    def step(g, carry):
        work(g)
        inner(g).start()
        return carry

    lax.fori_loop(1, ROLES * GROUPS, step, 0)

    partners = [pole, across, mate]
    names = [
        pltpu.make_async_remote_copy(
            src_ref=label, dst_ref=label_in.at[r],
            send_sem=z_send.at[ROLES * GROUPS + r], recv_sem=z_recv.at[ROLES * GROUPS + r],
            device_id={"horiz": partners[r]}, device_id_type=MESH,
        )
        for r in range(ROLES)
    ]
    for copy in names:
        copy.start()

    def halo(src, dst, n, target):
        return pltpu.make_async_remote_copy(
            src_ref=src, dst_ref=dst, send_sem=halo_send.at[n], recv_sem=halo_recv.at[n],
            device_id={"lev": target}, device_id_type=MESH,
        )

    slot_halo = [halo(slot_dn, slot_dn_in, 0, down), halo(slot_up, slot_up_in, 1, up)]
    for copy in slot_halo:
        copy.start()

    def own(t, carry):
        horizontal(t, t, h_own, tiles)
        return carry

    lax.fori_loop(0, tiles, own, 0, unroll=8)

    loads[2].wait()

    def displacement(b, carry):
        at = pl.multiple_of(b * 16, 16)
        for c in range(2):
            total = None
            for i in range(fl):
                term = adj32[pl.ds(pl.multiple_of(i * tiles + at, 16), 16), :] * traj[c, i, pl.ds(at, 16), :].astype(F32)
                total = term if total is None else total + term
            part[c, pl.ds(at, 16), :] = total
        return carry

    lax.fori_loop(0, tiles // 16, displacement, 0)
    span = tiles // flds
    short = span // levs

    def disp_copy(src, dst, n, axis, target):
        return pltpu.make_async_remote_copy(
            src_ref=src, dst_ref=dst, send_sem=disp_send.at[n], recv_sem=disp_recv.at[n],
            device_id={axis: target}, device_id_type=MESH,
        )

    to_x = []
    for d in range(1, flds):
        there = lax.rem(fld + d, flds)
        src = part.at[:, pl.ds(pl.multiple_of(there * span, span), span), :]
        to_x.append(disp_copy(src, part_x.at[d - 1], d - 1, "fld", there))
    for copy in to_x:
        copy.start()

    from_below = jnp.where(lev > 0, 1.0, 0.0).astype(F32)
    from_above = jnp.where(lev < levs - 1, 1.0, 0.0).astype(F32)
    for copy in slot_halo:
        copy.wait_recv()

    def edge_levels():
        for e in range(2):
            yield e, slot_up_in, own_up_in, from_below, e
            yield nl - 2 + e, slot_dn_in, own_dn_in, from_above, e

    outer = []
    for f in range(nf):
        for m, slots_in, _, keep, e in edge_levels():
            snd[f, m] = snd[f, m] + keep * slots_in[f, e]
            for r in range(ROLES):
                n = ROLES * GROUPS + ROLES + len(outer)
                piece = (f, m, pl.ds(r * CAP, CAP), slice(None))
                outer.append(pltpu.make_async_remote_copy(
                    src_ref=snd.at[piece], dst_ref=rcv.at[piece],
                    send_sem=z_send.at[n], recv_sem=z_recv.at[n],
                    device_id={"horiz": partners[r]}, device_id_type=MESH,
                ))
                outer[-1].start()

    def gather_own(i, carry):
        at = pl.ds(pl.multiple_of(i * tiles, tiles), tiles)
        h_own[at, :] = spread(own_hit, h_own[at, :])
        return carry

    lax.fori_loop(0, fl, gather_own, 0, unroll=2)

    def own_vertical(b, carry):
        at = pl.multiple_of(b * 8, 8)
        for f in range(nf):
            values = [h_own[pl.ds(pl.multiple_of((f * nl + l) * tiles + at, 8), 8), :] for l in range(nl)]

            def emit(e, value, f=f):
                if e < 2:
                    own_dn[f, e, pl.ds(at, 8), :] = value
                elif e < nl + 2:
                    acc[f, e - 2, pl.ds(at, 8), :] = value
                else:
                    own_up[f, e - nl - 2, pl.ds(at, 8), :] = value

            vertical(values, emit)
        return carry

    lax.fori_loop(0, tiles // 8, own_vertical, 0)
    own_halo = [halo(own_dn, own_dn_in, 2, down), halo(own_up, own_up_in, 3, up)]
    for copy in own_halo:
        copy.start()

    for copy in to_x:
        copy.wait_recv()
    mine = pl.multiple_of(fld * span, span)
    total = part[:, pl.ds(mine, span), :]
    for d in range(flds - 1):
        total = total + part_x[d]
    whole[:, pl.ds(mine, span), :] = total
    to_y = []
    for d in range(1, levs):
        there = lax.rem(lev + d, levs)
        src = whole.at[:, pl.ds(pl.multiple_of(mine + there * short, short), short), :]
        to_y.append(disp_copy(src, part_y.at[d - 1], 3 + d - 1, "lev", there))
    for copy in to_y:
        copy.start()
    for copy in to_y:
        copy.wait()
    piece = pl.multiple_of(mine + lev * short, short)
    total = whole[:, pl.ds(piece, short), :]
    for d in range(levs - 1):
        total = total + part_y[d]
    part[:, pl.ds(piece, short), :] = total
    back_y = []
    for copy in to_x:
        copy.wait_send()
    for d in range(1, levs):
        there = lax.rem(lev + d, levs)
        at = (slice(None), pl.ds(piece, short), slice(None))
        back_y.append(disp_copy(part.at[at], disp_ref.at[at], 6 + d - 1, "lev", there))
    for copy in back_y:
        copy.start()
    disp_ref[:, pl.ds(piece, short), :] = total
    for copy in back_y:
        copy.wait()
    back_x = []
    for d in range(1, flds):
        there = lax.rem(fld + d, flds)
        at = (slice(None), pl.ds(mine, span), slice(None))
        back_x.append(disp_copy(disp_ref.at[at], disp_ref.at[at], 9 + d - 1, "fld", there))
    for copy in back_x:
        copy.start()

    for copy in own_halo:
        copy.wait_recv()
    for f in range(nf):
        for m, _, own_in, keep, e in edge_levels():
            acc[f, m] = acc[f, m] + keep * own_in[f, e]

    for copy in names:
        copy.wait_recv()
    slot_lane = lax.broadcasted_iota(jnp.int32, (1, tiles), 1)
    arrived = jnp.where(slot_lane < CAP, label_in[0, 0:1], jnp.where(slot_lane < 2 * CAP, label_in[1, 0:1], label_in[2, 0:1]))
    arrived = jnp.where(slot_lane < SLOTS, arrived, -1)
    hit = jnp.where(jnp.broadcast_to(arrived, square) == row, 1.0, 0.0).astype(BF16)[:, :SLOTS]

    def store(f, m):
        return pltpu.make_async_copy(acc.at[f, m], out_hbm.at[f, m], out_sem.at[f, m])

    def wait_inner(g, carry):
        inner(g).wait_recv()
        return carry

    lax.fori_loop(0, ROLES * GROUPS, wait_inner, 0)

    def finish(m, carry):
        for f in range(nf):
            acc[f, m] = acc[f, m] + spread(hit, rcv[f, m])
            store(f, m).start()
        return carry

    lax.fori_loop(2, nl - 2, finish, 0)
    n = 0
    for f in range(nf):
        for m, _, _, _, _ in edge_levels():
            for r in range(ROLES):
                outer[n].wait_recv()
                n += 1
            acc[f, m] = acc[f, m] + spread(hit, rcv[f, m])
            store(f, m).start()

    for copy in back_x:
        copy.wait()

    def drain(g, carry):
        inner(g).wait_send()
        return carry

    lax.fori_loop(0, ROLES * GROUPS, drain, 0)
    for copy in outer + names + slot_halo + own_halo:
        copy.wait_send()

    def stored(m, carry):
        for f in range(nf):
            store(f, m).wait()
        return carry

    lax.fori_loop(0, nl, stored, 0)


def shards(mesh, adj_out, interp, vert_wts, vert_base, dep_tile, traj_grad):
    nf, nl, tiles, cols = adj_out.shape
    blocks, levs, flds = mesh.shape["horiz"], mesh.shape["lev"], mesh.shape["fld"]
    fl = nf * nl
    span = tiles // flds
    short = span // levs
    hbm = pl.BlockSpec(memory_space=pl.ANY)
    vmem = pl.BlockSpec(memory_space=pltpu.VMEM)
    smem = pl.BlockSpec(memory_space=pltpu.SMEM)
    n_z = ROLES * GROUPS + ROLES + ROLES * nf * 4
    n_disp = 2 * (flds - 1) + 2 * (levs - 1)
    dma = pltpu.SemaphoreType.DMA
    halo_slots = pltpu.VMEM((nf, 2, SLOTS, cols), F32)
    halo_own = pltpu.VMEM((nf, 2, tiles, cols), F32)
    field, disp = pl.pallas_call(
        functools.partial(kernel, blocks, levs, flds, nf, nl, tiles),
        out_shape=(
            jax.ShapeDtypeStruct((nf, nl, tiles, cols), F32),
            jax.ShapeDtypeStruct((2, tiles, cols), F32),
        ),
        in_specs=[hbm, hbm, hbm, vmem, smem, smem],
        out_specs=(hbm, vmem),
        scratch_shapes=[
            pltpu.VMEM((fl, tiles, cols), BF16),
            pltpu.VMEM((tiles, cols, cols), BF16),
            pltpu.VMEM((2, fl, tiles, cols), BF16),
            pltpu.VMEM((fl * tiles, cols), F32),
            pltpu.VMEM((fl * SLOTS, cols), F32),
            pltpu.VMEM((fl * tiles, cols), F32),
            pltpu.VMEM((nf, nl, SLOTS, cols), F32),
            pltpu.VMEM((nf, nl, SLOTS, cols), F32),
            halo_slots, halo_slots, halo_slots, halo_slots,
            halo_own, halo_own, halo_own, halo_own,
            pltpu.VMEM((nf, nl, tiles, cols), F32),
            pltpu.VMEM((8, tiles), jnp.int32),
            pltpu.VMEM((ROLES, 8, tiles), jnp.int32),
            pltpu.VMEM((8, tiles), jnp.int32),
            pltpu.SMEM((8, tiles), jnp.int32),
            pltpu.VMEM((2, tiles, cols), F32),
            pltpu.VMEM((flds - 1, 2, span, cols), F32),
            pltpu.VMEM((levs - 1, 2, short, cols), F32),
            pltpu.VMEM((2, tiles, cols), F32),
            dma((3,)), dma, dma((nf, nl)), dma((n_z,)), dma((n_z,)),
            dma((4,)), dma((4,)), dma((n_disp,)), dma((n_disp,)),
        ],
        compiler_params=pltpu.CompilerParams(
            collective_id=0, has_side_effects=True, vmem_limit_bytes=48 * 1024 * 1024
        ),
    )(
        adj_out.reshape(fl, tiles, cols), interp, traj_grad.reshape(2, fl, tiles, cols),
        dep_tile.reshape(1, tiles), vert_wts, vert_base,
    )
    return field, disp


def solution(mesh):
    return jax.shard_map(
        functools.partial(shards, mesh),
        mesh=mesh,
        in_specs=(
            P("fld", "lev", "horiz", None),
            P("horiz", None, None),
            P("lev", None),
            P("lev"),
            P("horiz"),
            P(None, "fld", "lev", "horiz", None),
        ),
        out_specs=(P("fld", "lev", "horiz", None), P(None, "horiz", None)),
        check_vma=False,
    )
```

time: 417 us -> 54.1 us (0.13)
  waiting for transfers between devices: 240 us -> 0 us
  other arithmetic: 111 us -> 0 us
  Pallas kernels: 0 us -> 46.4 us
  starting transfers between devices: 22.2 us -> 0 us
  between operations: 14.2 us -> 0.64 us
  local copies, waits for them, and re-layouts: 20.4 us -> 6.86 us
  matrix products: 7.9 us -> 0 us
    all_to_all x2 -> x0, waiting for transfers between devices: 154 us -> none  [the longest x1 154 us: shards(): lax.all_to_all(packed, 'horiz', split_axis=2, concat_axis=2, tiled=True)]
    scatter-add x4 -> x0, other arithmetic: 91.3 us -> none  [the longest x1 74.1 us: take_in(): padded = padded.at[:, :, ident, :].add(packed)]
    psum x1 -> x0, waiting for transfers between devices: 78.4 us -> none  [shards(): adj_disp = lax.psum(partial_disp, ('lev', 'fld'))]
    pallas_call x0 -> x1, Pallas kernels: none -> 46.4 us  [shards(): pl.pallas_call(functools.partial(kernel, blocks, levs, flds, nf, nl, tile...]
    all_to_all x2 -> x0, starting transfers between devices: 17.2 us -> none  [the longest x1 9.98 us: shards(): lax.all_to_all(labels, 'horiz', split_axis=2, concat_axis=2, tiled=True)]
    convert_element_type x3 -> x0, other arithmetic: 9.15 us -> none  [the longest x1 9.13 us: take_in(): ident = labels.reshape(-1).astype(jnp.int32)]
    gather x2 -> x0, local copies, waits for them, and re-layouts: 7.72 us -> none  [the longest x1 4.38 us: pack_slots(): packed = jnp.take(horiz, source, axis=2, mode='fill', fill_value=0.0)]
    select_n x6 -> x0, other arithmetic: 7.04 us -> none  [the longest x1 6.25 us: pack_slots(): packed = jnp.take(horiz, source, axis=2, mode='fill', fill_value=0.0)]
  transfers between devices with their start and end apart: 5 -> 0, of which waited for: 4 -> 0; matrix products, arithmetic and copies ran while one was open for 11% -> 0% of each run, Pallas kernels for 0% -> 0%
where the time goes in v1:
time: 54.1 us; the launch traced here: 53.9 us
  Pallas kernels  46.4 us (86%)
  local copies, waits for them, and re-layouts  6.86 us (13%)
  between operations  0.64 us (1%)
    pallas_call x1, Pallas kernels, shards(): pl.pallas_call(functools.partial(kernel, blocks, levs, flds, nf, nl, tile...  46.4 us
    unnamed x11, local copies, waits for them, and re-layouts  6.86 us

profile of v1, /device:TPU:1, one launch (start us, length us, event | category | flops | bytes accessed | tf_op | source)
XLA Modules:
  0.0 53.9 jit_solution(2800730425443780288)
XLA Ops:
  0.6 0.8 %copy.8.wts_ref = f32[16,4]{1,0:T(8,128)S(1)} copy(f32[16,4]{0,1:T(4,128)} %param.8) | data formatting | bytes 512 | tf_op args[2]
  1.4 0.0 copy-start
  1.4 1.6 %copy-done = bf16[2,2,16,128,128]{4,3,2,1,0:T(8,128)(2,1)S(1)} copy-done((bf16[2,2,16,128,128]{4,3,2,1,0:T(8,128)(2,1)S(1)}, bf16[2,2,16,128,128]{4,3,2,1,0:T(8,128)(2,1)}, u32[]{:S(2)}) %copy-start) | copy-done | bytes 2097176
  3.0 0.0 copy-start.1
  3.0 1.2 %copy-done.1 = bf16[2,16,128,128]{3,2,1,0:T(8,128)(2,1)S(1)} copy-done((bf16[2,16,128,128]{3,2,1,0:T(8,128)(2,1)S(1)}, bf16[2,16,128,128]{3,2,1,0:T(8,128)(2,1)}, u32[]{:S(2)}) %copy-start.1) | copy-done | bytes 1048600
  4.2 0.0 copy-start.2
  4.2 0.7 %copy-done.2 = s32[128]{0:T(128)S(1)} copy-done((s32[128]{0:T(128)S(1)}, s32[128]{0:T(128)}, u32[]{:S(2)}) %copy-start.2) | copy-done | bytes 536
  4.9 0.0 copy-start.3
  4.9 0.7 %copy-done.3 = s32[16]{0:T(128)S(1)} copy-done((s32[16]{0:T(128)S(1)}, s32[16]{0:T(128)}, u32[]{:S(2)}) %copy-start.3) | copy-done | bytes 88
  5.5 46.4 %shard_map.77 = (f32[2,16,128,128]{3,2,1,0:T(8,128)S(1)}, f32[2,128,128]{2,1,0:T(8,128)S(1)}) custom-call(bf16[32,128,128]{2,1,0:T(8,128)(2,1)S(1)} %bitcast.4, bf16[128,128,128]{2,1,0:T(8,128)(2,1)} %interp_hbm.1, bf16[2,32,128,128]{3,2,1,0:T(8,128)(2,1)S(1)} %bitcast.3, s32[1,128]{1,0:T(1,128)S(1)} %bitcast.5, f32[16,4]{1,0:T(8,128)S(1)} %copy.8.wts_ref, ...), custom_call_target="tpu_custom_call" | custom-call | tf_op jit(solution)/shard_map/pallas_call | solution.py:382
  51.9 1.3 %copy.11 = f32[2,16,128,128]{3,2,1,0:T(8,128)} copy(f32[2,16,128,128]{3,2,1,0:T(8,128)S(1)} %get-tuple-element.4) | data formatting | bytes 4194304
  53.2 0.7 %copy.12 = f32[2,128,128]{2,1,0:T(8,128)} copy(f32[2,128,128]{2,1,0:T(8,128)S(1)} %get-tuple-element.5) | data formatting | bytes 262144
Async XLA Ops:
  1.4 1.6 %copy-start = (bf16[2,2,16,128,128]{4,3,2,1,0:T(8,128)(2,1)S(1)}, bf16[2,2,16,128,128]{4,3,2,1,0:T(8,128)(2,1)}, u32[]{:S(2)}) copy-start(bf16[2,2,16,128,128]{4,3,2,1,0:T(8,128)(2,1)} %param.11) | copy-start | bytes 6291460
  3.0 1.2 %copy-start.1 = (bf16[2,16,128,128]{3,2,1,0:T(8,128)(2,1)S(1)}, bf16[2,16,128,128]{3,2,1,0:T(8,128)(2,1)}, u32[]{:S(2)}) copy-start(bf16[2,16,128,128]{3,2,1,0:T(8,128)(2,1)} %param.6) | copy-start | bytes 3145732
  4.2 0.7 %copy-start.2 = (s32[128]{0:T(128)S(1)}, s32[128]{0:T(128)}, u32[]{:S(2)}) copy-start(s32[128]{0:T(128)} %param.10) | copy-start | bytes 1540
  4.9 0.7 %copy-start.3 = (s32[16]{0:T(128)S(1)}, s32[16]{0:T(128)}, u32[]{:S(2)}) copy-start(s32[16]{0:T(128)} %base_ref.1) | copy-start | bytes 196

commit v2 on v1

--- a/solution.py
+++ b/solution.py
@@ -13,6 +13,7 @@
 GROUP = 8
 GROUPS = CAP // GROUP
 SLOTS = ROLES * CAP
+VMEM_BYTES = 48 * 1024 * 1024
 F32, BF16 = jnp.float32, jnp.bfloat16
 
 
@@ -30,12 +31,12 @@
 
 def kernel(
     blocks, levs, flds, nf, nl, tiles,
-    adj_hbm, interp_hbm, traj_hbm, dep_ref, wts_ref, base_ref,
-    out_hbm, disp_ref,
+    adj_hbm, interp_hbm, traj_hbm, dep_hbm, wts_hbm, base_hbm,
+    acc, disp_ref,
     adj, interp, traj, adj32, h_slot, h_own, snd, rcv,
     slot_dn, slot_up, slot_dn_in, slot_up_in, own_dn, own_up, own_dn_in, own_up_in,
-    acc, label, label_in, index_v, index_s, part, part_x, part_y, whole,
-    in_sem, index_sem, out_sem, z_send, z_recv, halo_send, halo_recv, disp_send, disp_recv,
+    dep_ref, wts_ref, base_ref, label, label_in, index_v, index_s, part, part_x, part_y, whole,
+    in_sem, index_sem, z_send, z_recv, halo_send, halo_recv, disp_send, disp_recv,
 ):
     fl = nf * nl
     here, lev, fld = lax.axis_index("horiz"), lax.axis_index("lev"), lax.axis_index("fld")
@@ -45,12 +46,12 @@
     mate = here + 1 - 2 * core
     up, down = lax.rem(lev + 1, levs), lax.rem(lev + levs - 1, levs)
 
-    loads = [
-        pltpu.make_async_copy(adj_hbm, adj, in_sem.at[0]),
-        pltpu.make_async_copy(interp_hbm, interp, in_sem.at[1]),
-        pltpu.make_async_copy(traj_hbm, traj, in_sem.at[2]),
+    pairs = [
+        (dep_hbm, dep_ref), (wts_hbm, wts_ref), (base_hbm, base_ref),
+        (adj_hbm, adj), (interp_hbm, interp), (traj_hbm, traj),
     ]
-    for load in loads:
+    loads = [pltpu.make_async_copy(src, dst, in_sem.at[i]) for i, (src, dst) in enumerate(pairs)]
+    for load in loads[:5]:
         load.start()
 
     barrier = pltpu.get_barrier_semaphore()
@@ -60,6 +61,7 @@
     for peer in peers:
         pl.semaphore_signal(barrier, inc=1, device_id=peer, device_id_type=MESH)
 
+    loads[0].wait()
     square = (tiles, tiles)
     by_lane = jnp.broadcast_to(dep_ref[...], square)
     by_row = by_lane.T
@@ -84,10 +86,12 @@
     own_hit = jnp.where((lane_role == ROLES) & (lax.rem(by_lane, tiles) == row), 1.0, 0.0).astype(BF16)
 
     first = lev * nl
+    loads[1].wait()
+    loads[2].wait()
     coef = []
     for l in range(nl):
         late = base_ref[l] < first + l
-        taps = [wts_ref[l, j] for j in range(4)]
+        taps = [wts_ref[j, l] for j in range(4)]
         coef.append([
             jnp.where(late, taps[k] if k < 4 else 0.0, taps[k - 1] if k > 0 else 0.0) for k in range(5)
         ])
@@ -100,7 +104,7 @@
                 total = term if total is None else total + term
             emit(e, total)
 
-    loads[0].wait()
+    loads[3].wait()
 
     def widen(i, carry):
         adj32[pl.ds(pl.multiple_of(i * tiles, tiles), tiles), :] = adj[i].astype(F32)
@@ -108,7 +112,8 @@
 
     lax.fori_loop(0, fl, widen, 0)
     index_copy.wait()
-    loads[1].wait()
+    loads[4].wait()
+    loads[5].start()
 
     def horizontal(t, s, dest, extent):
         rows = [adj32[pl.ds(t + b * 8 * tiles, 8, stride=tiles), :] for b in range(fl // 8)]
@@ -185,7 +190,7 @@
 
     lax.fori_loop(0, tiles, own, 0, unroll=8)
 
-    loads[2].wait()
+    loads[5].wait()
 
     def displacement(b, carry):
         at = pl.multiple_of(b * 16, 16)
@@ -321,9 +326,6 @@
     arrived = jnp.where(slot_lane < SLOTS, arrived, -1)
     hit = jnp.where(jnp.broadcast_to(arrived, square) == row, 1.0, 0.0).astype(BF16)[:, :SLOTS]
 
-    def store(f, m):
-        return pltpu.make_async_copy(acc.at[f, m], out_hbm.at[f, m], out_sem.at[f, m])
-
     def wait_inner(g, carry):
         inner(g).wait_recv()
         return carry
@@ -333,7 +335,6 @@
     def finish(m, carry):
         for f in range(nf):
             acc[f, m] = acc[f, m] + spread(hit, rcv[f, m])
-            store(f, m).start()
         return carry
 
     lax.fori_loop(2, nl - 2, finish, 0)
@@ -344,7 +345,6 @@
                 outer[n].wait_recv()
                 n += 1
             acc[f, m] = acc[f, m] + spread(hit, rcv[f, m])
-            store(f, m).start()
 
     for copy in back_x:
         copy.wait()
@@ -357,12 +357,16 @@
     for copy in outer + names + slot_halo + own_halo:
         copy.wait_send()
 
-    def stored(m, carry):
-        for f in range(nf):
-            store(f, m).wait()
-        return carry
-
-    lax.fori_loop(0, nl, stored, 0)
+
+def deliver(field_ref, disp_ref, field_out, disp_out, sem):
+    copies = [
+        pltpu.make_async_copy(field_ref, field_out, sem.at[0]),
+        pltpu.make_async_copy(disp_ref, disp_out, sem.at[1]),
+    ]
+    for copy in copies:
+        copy.start()
+    for copy in copies:
+        copy.wait()
 
 
 def shards(mesh, adj_out, interp, vert_wts, vert_base, dep_tile, traj_grad):
@@ -373,7 +377,6 @@
     short = span // levs
     hbm = pl.BlockSpec(memory_space=pl.ANY)
     vmem = pl.BlockSpec(memory_space=pltpu.VMEM)
-    smem = pl.BlockSpec(memory_space=pltpu.SMEM)
     n_z = ROLES * GROUPS + ROLES + ROLES * nf * 4
     n_disp = 2 * (flds - 1) + 2 * (levs - 1)
     dma = pltpu.SemaphoreType.DMA
@@ -382,11 +385,11 @@
     field, disp = pl.pallas_call(
         functools.partial(kernel, blocks, levs, flds, nf, nl, tiles),
         out_shape=(
-            jax.ShapeDtypeStruct((nf, nl, tiles, cols), F32),
-            jax.ShapeDtypeStruct((2, tiles, cols), F32),
+            pltpu.VMEM((nf, nl, tiles, cols), F32),
+            pltpu.VMEM((2, tiles, cols), F32),
         ),
-        in_specs=[hbm, hbm, hbm, vmem, smem, smem],
-        out_specs=(hbm, vmem),
+        in_specs=[hbm] * 6,
+        out_specs=(vmem, vmem),
         scratch_shapes=[
             pltpu.VMEM((fl, tiles, cols), BF16),
             pltpu.VMEM((tiles, cols, cols), BF16),
@@ -398,7 +401,9 @@
             pltpu.VMEM((nf, nl, SLOTS, cols), F32),
             halo_slots, halo_slots, halo_slots, halo_slots,
             halo_own, halo_own, halo_own, halo_own,
-            pltpu.VMEM((nf, nl, tiles, cols), F32),
+            pltpu.VMEM((1, tiles), jnp.int32),
+            pltpu.SMEM((4, nl), F32),
+            pltpu.SMEM((nl,), jnp.int32),
             pltpu.VMEM((8, tiles), jnp.int32),
             pltpu.VMEM((ROLES, 8, tiles), jnp.int32),
             pltpu.VMEM((8, tiles), jnp.int32),
@@ -407,17 +412,26 @@
             pltpu.VMEM((flds - 1, 2, span, cols), F32),
             pltpu.VMEM((levs - 1, 2, short, cols), F32),
             pltpu.VMEM((2, tiles, cols), F32),
-            dma((3,)), dma, dma((nf, nl)), dma((n_z,)), dma((n_z,)),
+            dma((6,)), dma, dma((n_z,)), dma((n_z,)),
             dma((4,)), dma((4,)), dma((n_disp,)), dma((n_disp,)),
         ],
         compiler_params=pltpu.CompilerParams(
-            collective_id=0, has_side_effects=True, vmem_limit_bytes=48 * 1024 * 1024
+            collective_id=0, has_side_effects=True, vmem_limit_bytes=VMEM_BYTES
         ),
-    )(
-        adj_out.reshape(fl, tiles, cols), interp, traj_grad.reshape(2, fl, tiles, cols),
-        dep_tile.reshape(1, tiles), vert_wts, vert_base,
-    )
-    return field, disp
+    )(*[
+        pltpu.with_memory_space_constraint(x, pltpu.HBM)
+        for x in (
+            adj_out.reshape(fl, tiles, cols), interp, traj_grad.reshape(2, fl, tiles, cols),
+            dep_tile.reshape(1, tiles), vert_wts.T, vert_base,
+        )
+    ])
+    return pl.pallas_call(
+        deliver,
+        out_shape=(pltpu.HBM(field.shape, F32), pltpu.HBM(disp.shape, F32)),
+        in_specs=[vmem] * 2,
+        out_specs=(hbm, hbm),
+        scratch_shapes=[dma((2,))],
+    )(*[pltpu.with_memory_space_constraint(x, pltpu.VMEM) for x in (field, disp)])
 
 
 def solution(mesh):

time: 54.1 us -> 43 us (0.79)
  local copies, waits for them, and re-layouts: 6.86 us -> 0 us
  Pallas kernels: 46.4 us -> 42.3 us
    unnamed x11 -> x0, local copies, waits for them, and re-layouts: 6.86 us -> none
    pallas_call x1, Pallas kernels: 46.4 us -> 40.9 us  [shards(): pl.pallas_call(functools.partial(kernel, blocks, levs, flds, nf, nl, tile...]
    pallas_call x0 -> x1, Pallas kernels: none -> 1.36 us  [shards(): pl.pallas_call(deliver, out_shape=(pltpu.HBM(field.shape, F32), pltpu.HBM...]
where the time goes in v2:
time: 43 us; the launch traced here: 42.9 us
  Pallas kernels  42.3 us (98%)
  between operations  0.64 us (1%)
    pallas_call x1, Pallas kernels, shards(): pl.pallas_call(functools.partial(kernel, blocks, levs, flds, nf, nl, tile...  40.9 us
    pallas_call x1, Pallas kernels, shards(): pl.pallas_call(deliver, out_shape=(pltpu.HBM(field.shape, F32), pltpu.HBM...  1.36 us

profile of v2, /device:TPU:1, one launch (start us, length us, event | category | flops | bytes accessed | tf_op | source)
XLA Modules:
  0.0 42.9 jit_solution(9789447903573896189)
XLA Ops:
  0.6 40.9 %shard_map.77 = (f32[2,16,128,128]{3,2,1,0:T(8,128)S(1)}, f32[2,128,128]{2,1,0:T(8,128)S(1)}) custom-call(bf16[32,128,128]{2,1,0:T(8,128)(2,1)} %bitcast.5, bf16[128,128,128]{2,1,0:T(8,128)(2,1)} %interp_hbm.1, bf16[2,32,128,128]{3,2,1,0:T(8,128)(2,1)} %bitcast.4, s32[1,128]{1,0:T(1,128)} %bitcast.7, f32[4,16]{1,0:T(4,128)} %bitcast.6, s32[16]{0:T(128)} %base_hbm.1), custom_call_target="tpu_custom_call" | custom-call | tf_op jit(solution)/shard_map/pallas_call | solution.py:385
  41.6 1.4 %shard_map.78 = (f32[2,16,128,128]{3,2,1,0:T(8,128)}, f32[2,128,128]{2,1,0:T(8,128)}) custom-call(f32[2,16,128,128]{3,2,1,0:T(8,128)S(1)} %get-tuple-element.4.field_ref, f32[2,128,128]{2,1,0:T(8,128)S(1)} %get-tuple-element.5.disp_ref), custom_call_target="tpu_custom_call" | custom-call | tf_op jit(solution)/shard_map/pallas_call | solution.py:428

commit v3 on v2

--- a/solution.py
+++ b/solution.py
@@ -34,9 +34,9 @@
     adj_hbm, interp_hbm, traj_hbm, dep_hbm, wts_hbm, base_hbm,
     acc, disp_ref,
     adj, interp, traj, adj32, h_slot, h_own, snd, rcv,
-    slot_dn, slot_up, slot_dn_in, slot_up_in, own_dn, own_up, own_dn_in, own_up_in,
+    slot_edge, slot_edge_in, own_edge, own_edge_in,
     dep_ref, wts_ref, base_ref, label, label_in, index_v, index_s, part, part_x, part_y, whole,
-    in_sem, index_sem, z_send, z_recv, halo_send, halo_recv, disp_send, disp_recv,
+    in_sem, index_sem, answered, name_sem, z_send, z_recv, halo_send, halo_recv, disp_send, disp_recv,
 ):
     fl = nf * nl
     here, lev, fld = lax.axis_index("horiz"), lax.axis_index("lev"), lax.axis_index("fld")
@@ -44,6 +44,7 @@
     pole = lax.rem(here + blocks // 2, blocks)
     across = lax.rem(here + 2 * core - 1 + blocks, blocks)
     mate = here + 1 - 2 * core
+    next_x = lax.rem(fld + 1, flds)
     up, down = lax.rem(lev + 1, levs), lax.rem(lev + levs - 1, levs)
 
     pairs = [
@@ -55,11 +56,15 @@
         load.start()
 
     barrier = pltpu.get_barrier_semaphore()
-    peers = [{"horiz": pole}, {"horiz": across}, {"horiz": mate}]
-    peers += [{"lev": lax.rem(lev + d, levs)} for d in range(1, levs)]
-    peers += [{"fld": lax.rem(fld + d, flds)} for d in range(1, flds)]
-    for peer in peers:
-        pl.semaphore_signal(barrier, inc=1, device_id=peer, device_id_type=MESH)
+    partners = [pole, across, mate]
+    for partner in partners:
+        pl.semaphore_signal(barrier, inc=1, device_id={"horiz": partner}, device_id_type=MESH)
+    for axis, me, size in (("lev", lev, levs), ("fld", fld, flds)):
+        for d in range(1, size):
+
+            @pl.when(me + d < size)
+            def _(axis=axis, me=me, d=d):
+                pl.semaphore_signal(barrier, inc=1, device_id={axis: me + d}, device_id_type=MESH)
 
     loads[0].wait()
     square = (tiles, tiles)
@@ -80,7 +85,8 @@
     source = jnp.sum(jnp.where(chosen, row, 0), axis=0, keepdims=True)
     target = jnp.sum(jnp.where(chosen, lax.rem(by_row, tiles) + 1, 0), axis=0, keepdims=True) - 1
     index_v[...] = jnp.broadcast_to(source, index_v.shape)
-    label[...] = jnp.broadcast_to(target, label.shape)
+    for r in range(ROLES):
+        label[r] = jnp.broadcast_to(target, label.shape[1:])
     index_copy = pltpu.make_async_copy(index_v, index_s, index_sem)
     index_copy.start()
     own_hit = jnp.where((lane_role == ROLES) & (lax.rem(by_lane, tiles) == row), 1.0, 0.0).astype(BF16)
@@ -132,11 +138,11 @@
 
             def emit(e, value, f=f):
                 if e < 2:
-                    slot_dn[f, e, pl.ds(at, GROUP), :] = value
+                    slot_edge[0, f, e, pl.ds(at, GROUP), :] = value
                 elif e < nl + 2:
                     snd[f, e - 2, pl.ds(at, GROUP), :] = value
                 else:
-                    slot_up[f, e - nl - 2, pl.ds(at, GROUP), :] = value
+                    slot_edge[1, f, e - nl - 2, pl.ds(at, GROUP), :] = value
 
             vertical(values, emit)
 
@@ -147,48 +153,27 @@
         piece = (slice(None), pl.ds(2, nl - 4), pl.ds(at, GROUP), slice(None))
         return pltpu.make_async_remote_copy(
             src_ref=snd.at[piece], dst_ref=rcv.at[piece],
-            send_sem=z_send.at[g], recv_sem=z_recv.at[g],
+            send_sem=z_send, recv_sem=z_recv.at[0],
             device_id={"horiz": partner}, device_id_type=MESH,
         )
 
     work(0)
-    pl.semaphore_wait(barrier, len(peers))
+    pl.semaphore_wait(barrier, ROLES + lev + fld)
     inner(0).start()
+    for axis, me, size in (("lev", lev, levs), ("fld", fld, flds)):
+        for d in range(1, size):
+
+            @pl.when(me >= d)
+            def _(axis=axis, me=me, d=d):
+                pl.semaphore_signal(answered, inc=1, device_id={axis: me - d}, device_id_type=MESH)
+
 
     def step(g, carry):
         work(g)
         inner(g).start()
         return carry
 
-    lax.fori_loop(1, ROLES * GROUPS, step, 0)
-
-    partners = [pole, across, mate]
-    names = [
-        pltpu.make_async_remote_copy(
-            src_ref=label, dst_ref=label_in.at[r],
-            send_sem=z_send.at[ROLES * GROUPS + r], recv_sem=z_recv.at[ROLES * GROUPS + r],
-            device_id={"horiz": partners[r]}, device_id_type=MESH,
-        )
-        for r in range(ROLES)
-    ]
-    for copy in names:
-        copy.start()
-
-    def halo(src, dst, n, target):
-        return pltpu.make_async_remote_copy(
-            src_ref=src, dst_ref=dst, send_sem=halo_send.at[n], recv_sem=halo_recv.at[n],
-            device_id={"lev": target}, device_id_type=MESH,
-        )
-
-    slot_halo = [halo(slot_dn, slot_dn_in, 0, down), halo(slot_up, slot_up_in, 1, up)]
-    for copy in slot_halo:
-        copy.start()
-
-    def own(t, carry):
-        horizontal(t, t, h_own, tiles)
-        return carry
-
-    lax.fori_loop(0, tiles, own, 0, unroll=8)
+    lax.fori_loop(1, GROUPS, step, 0)
 
     loads[5].wait()
 
@@ -212,68 +197,55 @@
             device_id={axis: target}, device_id_type=MESH,
         )
 
+    def disp_all(like, n, axis):
+        return disp_copy(like, like, n, axis, next_x if axis == "fld" else up)
+
     to_x = []
     for d in range(1, flds):
         there = lax.rem(fld + d, flds)
         src = part.at[:, pl.ds(pl.multiple_of(there * span, span), span), :]
-        to_x.append(disp_copy(src, part_x.at[d - 1], d - 1, "fld", there))
+        to_x.append(disp_copy(src, part_x.at[d - 1], 0, "fld", there))
+    answers = levs - 1 - lev + flds - 1 - fld
+
+    @pl.when(answers > 0)
+    def _():
+        pl.semaphore_wait(answered, answers)
+
     for copy in to_x:
         copy.start()
 
-    from_below = jnp.where(lev > 0, 1.0, 0.0).astype(F32)
-    from_above = jnp.where(lev < levs - 1, 1.0, 0.0).astype(F32)
+    lax.fori_loop(GROUPS, ROLES * GROUPS, step, 0)
+
+    names = [
+        pltpu.make_async_remote_copy(
+            src_ref=label.at[r], dst_ref=label_in.at[r], send_sem=name_sem.at[0], recv_sem=name_sem.at[1],
+            device_id={"horiz": partners[r]}, device_id_type=MESH,
+        )
+        for r in range(ROLES)
+    ]
+    for copy in names:
+        copy.start()
+
+    def halo(src, dst, n):
+        return [
+            pltpu.make_async_remote_copy(
+                src_ref=src.at[way], dst_ref=dst.at[way], send_sem=halo_send.at[n], recv_sem=halo_recv.at[n],
+                device_id={"lev": target}, device_id_type=MESH,
+            )
+            for way, target in enumerate((down, up))
+        ]
+
+    def halo_both(src, dst, n):
+        return pltpu.make_async_remote_copy(
+            src_ref=src, dst_ref=dst, send_sem=halo_send.at[n], recv_sem=halo_recv.at[n],
+            device_id={"lev": up}, device_id_type=MESH,
+        )
+
+    slot_halo = halo(slot_edge, slot_edge_in, 0)
     for copy in slot_halo:
-        copy.wait_recv()
-
-    def edge_levels():
-        for e in range(2):
-            yield e, slot_up_in, own_up_in, from_below, e
-            yield nl - 2 + e, slot_dn_in, own_dn_in, from_above, e
-
-    outer = []
-    for f in range(nf):
-        for m, slots_in, _, keep, e in edge_levels():
-            snd[f, m] = snd[f, m] + keep * slots_in[f, e]
-            for r in range(ROLES):
-                n = ROLES * GROUPS + ROLES + len(outer)
-                piece = (f, m, pl.ds(r * CAP, CAP), slice(None))
-                outer.append(pltpu.make_async_remote_copy(
-                    src_ref=snd.at[piece], dst_ref=rcv.at[piece],
-                    send_sem=z_send.at[n], recv_sem=z_recv.at[n],
-                    device_id={"horiz": partners[r]}, device_id_type=MESH,
-                ))
-                outer[-1].start()
-
-    def gather_own(i, carry):
-        at = pl.ds(pl.multiple_of(i * tiles, tiles), tiles)
-        h_own[at, :] = spread(own_hit, h_own[at, :])
-        return carry
-
-    lax.fori_loop(0, fl, gather_own, 0, unroll=2)
-
-    def own_vertical(b, carry):
-        at = pl.multiple_of(b * 8, 8)
-        for f in range(nf):
-            values = [h_own[pl.ds(pl.multiple_of((f * nl + l) * tiles + at, 8), 8), :] for l in range(nl)]
-
-            def emit(e, value, f=f):
-                if e < 2:
-                    own_dn[f, e, pl.ds(at, 8), :] = value
-                elif e < nl + 2:
-                    acc[f, e - 2, pl.ds(at, 8), :] = value
-                else:
-                    own_up[f, e - nl - 2, pl.ds(at, 8), :] = value
-
-            vertical(values, emit)
-        return carry
-
-    lax.fori_loop(0, tiles // 8, own_vertical, 0)
-    own_halo = [halo(own_dn, own_dn_in, 2, down), halo(own_up, own_up_in, 3, up)]
-    for copy in own_halo:
-        copy.start()
-
-    for copy in to_x:
-        copy.wait_recv()
+        copy.start()
+
+    disp_all(part_x, 0, "fld").wait_recv()
     mine = pl.multiple_of(fld * span, span)
     total = part[:, pl.ds(mine, span), :]
     for d in range(flds - 1):
@@ -283,54 +255,115 @@
     for d in range(1, levs):
         there = lax.rem(lev + d, levs)
         src = whole.at[:, pl.ds(pl.multiple_of(mine + there * short, short), short), :]
-        to_y.append(disp_copy(src, part_y.at[d - 1], 3 + d - 1, "lev", there))
+        to_y.append(disp_copy(src, part_y.at[d - 1], 1, "lev", there))
     for copy in to_y:
         copy.start()
-    for copy in to_y:
-        copy.wait()
+
+    def own(t, carry):
+        horizontal(t, t, h_own, tiles)
+        return carry
+
+    lax.fori_loop(0, tiles // 2, own, 0, unroll=8)
+
+    disp_all(part_y, 1, "lev").wait()
     piece = pl.multiple_of(mine + lev * short, short)
     total = whole[:, pl.ds(piece, short), :]
     for d in range(levs - 1):
         total = total + part_y[d]
     part[:, pl.ds(piece, short), :] = total
     back_y = []
-    for copy in to_x:
-        copy.wait_send()
+    disp_all(part_x, 0, "fld").wait_send()
     for d in range(1, levs):
         there = lax.rem(lev + d, levs)
         at = (slice(None), pl.ds(piece, short), slice(None))
-        back_y.append(disp_copy(part.at[at], disp_ref.at[at], 6 + d - 1, "lev", there))
+        back_y.append(disp_copy(part.at[at], disp_ref.at[at], 2, "lev", there))
     for copy in back_y:
         copy.start()
     disp_ref[:, pl.ds(piece, short), :] = total
-    for copy in back_y:
-        copy.wait()
+
+    lax.fori_loop(tiles // 2, tiles, own, 0, unroll=8)
+
+    disp_all(part_y, 2, "lev").wait()
     back_x = []
     for d in range(1, flds):
         there = lax.rem(fld + d, flds)
         at = (slice(None), pl.ds(mine, span), slice(None))
-        back_x.append(disp_copy(disp_ref.at[at], disp_ref.at[at], 9 + d - 1, "fld", there))
+        back_x.append(disp_copy(disp_ref.at[at], disp_ref.at[at], 3, "fld", there))
     for copy in back_x:
         copy.start()
 
+
+    from_below = jnp.where(lev > 0, 1.0, 0.0).astype(F32)
+    from_above = jnp.where(lev < levs - 1, 1.0, 0.0).astype(F32)
+    halo_both(slot_edge, slot_edge_in, 0).wait_recv()
+
+    edges = ((0, 1, from_below), (nl - 2, 0, from_above))
+
+    def outer(f, low, r):
+        n = 1 + f * 2 + (0 if low == 0 else 1)
+        piece = (f, pl.ds(low, 2), pl.ds(r * CAP, CAP), slice(None))
+        return pltpu.make_async_remote_copy(
+            src_ref=snd.at[piece], dst_ref=rcv.at[piece],
+            send_sem=z_send, recv_sem=z_recv.at[n],
+            device_id={"horiz": partners[r]}, device_id_type=MESH,
+        )
+
+    for f in range(nf):
+        for low, way, keep in edges:
+            for e in range(2):
+                snd[f, low + e] = snd[f, low + e] + keep * slot_edge_in[way, f, e]
+            for r in range(ROLES):
+                outer(f, low, r).start()
+
+    def gather_own(i, carry):
+        at = pl.ds(pl.multiple_of(i * tiles, tiles), tiles)
+        h_own[at, :] = spread(own_hit, h_own[at, :])
+        return carry
+
+    lax.fori_loop(0, fl, gather_own, 0, unroll=2)
+
+    def own_vertical(b, carry):
+        at = pl.multiple_of(b * 8, 8)
+        for f in range(nf):
+            values = [h_own[pl.ds(pl.multiple_of((f * nl + l) * tiles + at, 8), 8), :] for l in range(nl)]
+
+            def emit(e, value, f=f):
+                if e < 2:
+                    own_edge[0, f, e, pl.ds(at, 8), :] = value
+                elif e < nl + 2:
+                    acc[f, e - 2, pl.ds(at, 8), :] = value
+                else:
+                    own_edge[1, f, e - nl - 2, pl.ds(at, 8), :] = value
+
+            vertical(values, emit)
+        return carry
+
+    lax.fori_loop(0, tiles // 8, own_vertical, 0)
+    own_halo = halo(own_edge, own_edge_in, 1)
     for copy in own_halo:
-        copy.wait_recv()
+        copy.start()
+
+    halo_both(own_edge, own_edge_in, 1).wait_recv()
     for f in range(nf):
-        for m, _, own_in, keep, e in edge_levels():
-            acc[f, m] = acc[f, m] + keep * own_in[f, e]
-
-    for copy in names:
-        copy.wait_recv()
+        for low, way, keep in edges:
+            for e in range(2):
+                acc[f, low + e] = acc[f, low + e] + keep * own_edge_in[way, f, e]
+
+    names_all = pltpu.make_async_remote_copy(
+        src_ref=label, dst_ref=label_in, send_sem=name_sem.at[0], recv_sem=name_sem.at[1],
+        device_id={"horiz": pole}, device_id_type=MESH,
+    )
+    names_all.wait_recv()
     slot_lane = lax.broadcasted_iota(jnp.int32, (1, tiles), 1)
     arrived = jnp.where(slot_lane < CAP, label_in[0, 0:1], jnp.where(slot_lane < 2 * CAP, label_in[1, 0:1], label_in[2, 0:1]))
     arrived = jnp.where(slot_lane < SLOTS, arrived, -1)
     hit = jnp.where(jnp.broadcast_to(arrived, square) == row, 1.0, 0.0).astype(BF16)[:, :SLOTS]
 
-    def wait_inner(g, carry):
-        inner(g).wait_recv()
-        return carry
-
-    lax.fori_loop(0, ROLES * GROUPS, wait_inner, 0)
+    whole_piece = (slice(None), pl.ds(2, nl - 4))
+    pltpu.make_async_remote_copy(
+        src_ref=snd.at[whole_piece], dst_ref=rcv.at[whole_piece], send_sem=z_send, recv_sem=z_recv.at[0],
+        device_id={"horiz": pole}, device_id_type=MESH,
+    ).wait_recv()
 
     def finish(m, carry):
         for f in range(nf):
@@ -338,24 +371,25 @@
         return carry
 
     lax.fori_loop(2, nl - 2, finish, 0)
-    n = 0
+
+    disp_all(part_x, 3, "fld").wait()
+    names_all.wait_send()
+    halo_both(slot_edge, slot_edge_in, 0).wait_send()
+    halo_both(own_edge, own_edge_in, 1).wait_send()
     for f in range(nf):
-        for m, _, _, _, _ in edge_levels():
-            for r in range(ROLES):
-                outer[n].wait_recv()
-                n += 1
-            acc[f, m] = acc[f, m] + spread(hit, rcv[f, m])
-
-    for copy in back_x:
-        copy.wait()
-
-    def drain(g, carry):
-        inner(g).wait_send()
-        return carry
-
-    lax.fori_loop(0, ROLES * GROUPS, drain, 0)
-    for copy in outer + names + slot_halo + own_halo:
-        copy.wait_send()
+        for low, _, _ in edges:
+            piece = (f, pl.ds(low, 2))
+            pltpu.make_async_remote_copy(
+                src_ref=snd.at[piece], dst_ref=rcv.at[piece], send_sem=z_send,
+                recv_sem=z_recv.at[1 + f * 2 + (0 if low == 0 else 1)],
+                device_id={"horiz": pole}, device_id_type=MESH,
+            ).wait_recv()
+            for e in range(2):
+                acc[f, low + e] = acc[f, low + e] + spread(hit, rcv[f, low + e])
+    pltpu.make_async_remote_copy(
+        src_ref=snd, dst_ref=rcv, send_sem=z_send, recv_sem=z_recv.at[0],
+        device_id={"horiz": pole}, device_id_type=MESH,
+    ).wait_send()
 
 
 def deliver(field_ref, disp_ref, field_out, disp_out, sem):
@@ -377,11 +411,9 @@
     short = span // levs
     hbm = pl.BlockSpec(memory_space=pl.ANY)
     vmem = pl.BlockSpec(memory_space=pltpu.VMEM)
-    n_z = ROLES * GROUPS + ROLES + ROLES * nf * 4
-    n_disp = 2 * (flds - 1) + 2 * (levs - 1)
     dma = pltpu.SemaphoreType.DMA
-    halo_slots = pltpu.VMEM((nf, 2, SLOTS, cols), F32)
-    halo_own = pltpu.VMEM((nf, 2, tiles, cols), F32)
+    halo_slots = pltpu.VMEM((2, nf, 2, SLOTS, cols), F32)
+    halo_own = pltpu.VMEM((2, nf, 2, tiles, cols), F32)
     field, disp = pl.pallas_call(
         functools.partial(kernel, blocks, levs, flds, nf, nl, tiles),
         out_shape=(
@@ -399,12 +431,11 @@
             pltpu.VMEM((fl * tiles, cols), F32),
             pltpu.VMEM((nf, nl, SLOTS, cols), F32),
             pltpu.VMEM((nf, nl, SLOTS, cols), F32),
-            halo_slots, halo_slots, halo_slots, halo_slots,
-            halo_own, halo_own, halo_own, halo_own,
+            halo_slots, halo_slots, halo_own, halo_own,
             pltpu.VMEM((1, tiles), jnp.int32),
             pltpu.SMEM((4, nl), F32),
             pltpu.SMEM((nl,), jnp.int32),
-            pltpu.VMEM((8, tiles), jnp.int32),
+            pltpu.VMEM((ROLES, 8, tiles), jnp.int32),
             pltpu.VMEM((ROLES, 8, tiles), jnp.int32),
             pltpu.VMEM((8, tiles), jnp.int32),
             pltpu.SMEM((8, tiles), jnp.int32),
@@ -412,8 +443,8 @@
             pltpu.VMEM((flds - 1, 2, span, cols), F32),
             pltpu.VMEM((levs - 1, 2, short, cols), F32),
             pltpu.VMEM((2, tiles, cols), F32),
-            dma((6,)), dma, dma((n_z,)), dma((n_z,)),
-            dma((4,)), dma((4,)), dma((n_disp,)), dma((n_disp,)),
+            dma((6,)), dma, pltpu.SemaphoreType.REGULAR, dma((2,)), dma, dma((1 + 2 * nf,)),
+            dma((2,)), dma((2,)), dma((4,)), dma((4,)),
         ],
         compiler_params=pltpu.CompilerParams(
             collective_id=0, has_side_effects=True, vmem_limit_bytes=VMEM_BYTES

time: 43 us -> 41.7 us (0.970)
  Pallas kernels: 42.3 us -> 41 us
    pallas_call x1, Pallas kernels: 40.9 us -> 39.6 us  [shards(): pl.pallas_call(functools.partial(kernel, blocks, levs, flds, nf, nl, tile...]
where the time goes in v3:
time: 41.7 us; the launch traced here: 41.6 us
  Pallas kernels  41 us (98%)
  between operations  0.64 us (2%)
    pallas_call x1, Pallas kernels, shards(): pl.pallas_call(functools.partial(kernel, blocks, levs, flds, nf, nl, tile...  39.6 us
    pallas_call x1, Pallas kernels, shards(): pl.pallas_call(deliver, out_shape=(pltpu.HBM(field.shape, F32), pltpu.HBM...  1.36 us

profile of v3, /device:TPU:1, one launch (start us, length us, event | category | flops | bytes accessed | tf_op | source)
XLA Modules:
  0.0 41.6 jit_solution(8651852402266737983)
XLA Ops:
  0.6 39.6 %shard_map.77 = (f32[2,16,128,128]{3,2,1,0:T(8,128)S(1)}, f32[2,128,128]{2,1,0:T(8,128)S(1)}) custom-call(bf16[32,128,128]{2,1,0:T(8,128)(2,1)} %bitcast.5, bf16[128,128,128]{2,1,0:T(8,128)(2,1)} %interp_hbm.1, bf16[2,32,128,128]{3,2,1,0:T(8,128)(2,1)} %bitcast.4, s32[1,128]{1,0:T(1,128)} %bitcast.7, f32[4,16]{1,0:T(4,128)} %bitcast.6, s32[16]{0:T(128)} %base_hbm.1), custom_call_target="tpu_custom_call" | custom-call | tf_op jit(solution)/shard_map/pallas_call | solution.py:417
  40.2 1.4 %shard_map.78 = (f32[2,16,128,128]{3,2,1,0:T(8,128)}, f32[2,128,128]{2,1,0:T(8,128)}) custom-call(f32[2,16,128,128]{3,2,1,0:T(8,128)S(1)} %get-tuple-element.4.field_ref, f32[2,128,128]{2,1,0:T(8,128)S(1)} %get-tuple-element.5.disp_ref), custom_call_target="tpu_custom_call" | custom-call | tf_op jit(solution)/shard_map/pallas_call | solution.py:459

commit v4 on v3

--- a/solution.py
+++ b/solution.py
@@ -14,6 +14,7 @@
 GROUPS = CAP // GROUP
 SLOTS = ROLES * CAP
 VMEM_BYTES = 48 * 1024 * 1024
+KEPT_LOW, KEPT_TOP = 4, 2
 F32, BF16 = jnp.float32, jnp.bfloat16
 
 
@@ -153,7 +154,7 @@
         piece = (slice(None), pl.ds(2, nl - 4), pl.ds(at, GROUP), slice(None))
         return pltpu.make_async_remote_copy(
             src_ref=snd.at[piece], dst_ref=rcv.at[piece],
-            send_sem=z_send, recv_sem=z_recv.at[0],
+            send_sem=z_send, recv_sem=z_recv.at[jnp.where(role == 0, 0, 1)],
             device_id={"horiz": partner}, device_id_type=MESH,
         )
 
@@ -173,7 +174,12 @@
         inner(g).start()
         return carry
 
-    lax.fori_loop(1, GROUPS, step, 0)
+    def both(g, carry):
+        step(GROUPS + g - 1, 0)
+        step(g, 0)
+        return carry
+
+    lax.fori_loop(1, GROUPS, both, 0)
 
     loads[5].wait()
 
@@ -214,7 +220,7 @@
     for copy in to_x:
         copy.start()
 
-    lax.fori_loop(GROUPS, ROLES * GROUPS, step, 0)
+    lax.fori_loop(2 * GROUPS - 1, ROLES * GROUPS, step, 0)
 
     names = [
         pltpu.make_async_remote_copy(
@@ -300,7 +306,7 @@
     edges = ((0, 1, from_below), (nl - 2, 0, from_above))
 
     def outer(f, low, r):
-        n = 1 + f * 2 + (0 if low == 0 else 1)
+        n = 2 + f * 2 + (0 if low == 0 else 1)
         piece = (f, pl.ds(low, 2), pl.ds(r * CAP, CAP), slice(None))
         return pltpu.make_async_remote_copy(
             src_ref=snd.at[piece], dst_ref=rcv.at[piece],
@@ -312,8 +318,19 @@
         for low, way, keep in edges:
             for e in range(2):
                 snd[f, low + e] = snd[f, low + e] + keep * slot_edge_in[way, f, e]
-            for r in range(ROLES):
+            for r in range(1, ROLES):
                 outer(f, low, r).start()
+
+    half = blocks // 4
+    place = here // 2
+    kept = jnp.where(lax.rem(place, half) < half // 2, 0, jnp.where(place < half, KEPT_LOW, KEPT_TOP))
+    pieces = [(f, low) for f in range(nf) for low, _, _ in edges]
+    for n, (f, low) in enumerate(pieces):
+
+        @pl.when(n < len(pieces) - kept)
+        def _(f=f, low=low):
+            outer(f, low, 0).start()
+
 
     def gather_own(i, carry):
         at = pl.ds(pl.multiple_of(i * tiles, tiles), tiles)
@@ -342,6 +359,20 @@
     own_halo = halo(own_edge, own_edge_in, 1)
     for copy in own_halo:
         copy.start()
+
+    def inner_all(role, roles):
+        piece = (slice(None), pl.ds(2, nl - 4), pl.ds(role * CAP, roles * CAP))
+        return pltpu.make_async_remote_copy(
+            src_ref=snd.at[piece], dst_ref=rcv.at[piece], send_sem=z_send, recv_sem=z_recv.at[role],
+            device_id={"horiz": pole}, device_id_type=MESH,
+        )
+
+    inner_all(0, 1).wait_recv()
+    for n, (f, low) in enumerate(pieces):
+
+        @pl.when(n >= len(pieces) - kept)
+        def _(f=f, low=low):
+            outer(f, low, 0).start()
 
     halo_both(own_edge, own_edge_in, 1).wait_recv()
     for f in range(nf):
@@ -359,11 +390,7 @@
     arrived = jnp.where(slot_lane < SLOTS, arrived, -1)
     hit = jnp.where(jnp.broadcast_to(arrived, square) == row, 1.0, 0.0).astype(BF16)[:, :SLOTS]
 
-    whole_piece = (slice(None), pl.ds(2, nl - 4))
-    pltpu.make_async_remote_copy(
-        src_ref=snd.at[whole_piece], dst_ref=rcv.at[whole_piece], send_sem=z_send, recv_sem=z_recv.at[0],
-        device_id={"horiz": pole}, device_id_type=MESH,
-    ).wait_recv()
+    inner_all(1, ROLES - 1).wait_recv()
 
     def finish(m, carry):
         for f in range(nf):
@@ -381,7 +408,7 @@
             piece = (f, pl.ds(low, 2))
             pltpu.make_async_remote_copy(
                 src_ref=snd.at[piece], dst_ref=rcv.at[piece], send_sem=z_send,
-                recv_sem=z_recv.at[1 + f * 2 + (0 if low == 0 else 1)],
+                recv_sem=z_recv.at[2 + f * 2 + (0 if low == 0 else 1)],
                 device_id={"horiz": pole}, device_id_type=MESH,
             ).wait_recv()
             for e in range(2):
@@ -443,7 +470,7 @@
             pltpu.VMEM((flds - 1, 2, span, cols), F32),
             pltpu.VMEM((levs - 1, 2, short, cols), F32),
             pltpu.VMEM((2, tiles, cols), F32),
-            dma((6,)), dma, pltpu.SemaphoreType.REGULAR, dma((2,)), dma, dma((1 + 2 * nf,)),
+            dma((6,)), dma, pltpu.SemaphoreType.REGULAR, dma((2,)), dma, dma((2 + 2 * nf,)),
             dma((2,)), dma((2,)), dma((4,)), dma((4,)),
         ],
         compiler_params=pltpu.CompilerParams(

time: 41.7 us -> 41.2 us (0.988)
  Pallas kernels: 41 us -> 40.5 us
    pallas_call x1, Pallas kernels: 39.6 us -> 39.1 us  [shards(): pl.pallas_call(functools.partial(kernel, blocks, levs, flds, nf, nl, tile...]
where the time goes in v4:
time: 41.2 us; the launch traced here: 41.1 us
  Pallas kernels  40.5 us (98%)
  between operations  0.64 us (2%)
    pallas_call x1, Pallas kernels, shards(): pl.pallas_call(functools.partial(kernel, blocks, levs, flds, nf, nl, tile...  39.1 us
    pallas_call x1, Pallas kernels, shards(): pl.pallas_call(deliver, out_shape=(pltpu.HBM(field.shape, F32), pltpu.HBM...  1.36 us

profile of v4, /device:TPU:1, one launch (start us, length us, event | category | flops | bytes accessed | tf_op | source)
XLA Modules:
  0.0 41.1 jit_solution(12207621805352016216)
XLA Ops:
  0.6 39.1 %shard_map.77 = (f32[2,16,128,128]{3,2,1,0:T(8,128)S(1)}, f32[2,128,128]{2,1,0:T(8,128)S(1)}) custom-call(bf16[32,128,128]{2,1,0:T(8,128)(2,1)} %bitcast.5, bf16[128,128,128]{2,1,0:T(8,128)(2,1)} %interp_hbm.1, bf16[2,32,128,128]{3,2,1,0:T(8,128)(2,1)} %bitcast.4, s32[1,128]{1,0:T(1,128)} %bitcast.7, f32[4,16]{1,0:T(4,128)} %bitcast.6, s32[16]{0:T(128)} %base_hbm.1), custom_call_target="tpu_custom_call" | custom-call | tf_op jit(solution)/shard_map/pallas_call | solution.py:444
  39.7 1.4 %shard_map.78 = (f32[2,16,128,128]{3,2,1,0:T(8,128)}, f32[2,128,128]{2,1,0:T(8,128)}) custom-call(f32[2,16,128,128]{3,2,1,0:T(8,128)S(1)} %get-tuple-element.4.field_ref, f32[2,128,128]{2,1,0:T(8,128)S(1)} %get-tuple-element.5.disp_ref), custom_call_target="tpu_custom_call" | custom-call | tf_op jit(solution)/shard_map/pallas_call | solution.py:486

commit v5 on v4

--- a/solution.py
+++ b/solution.py
@@ -37,7 +37,7 @@
     adj, interp, traj, adj32, h_slot, h_own, snd, rcv,
     slot_edge, slot_edge_in, own_edge, own_edge_in,
     dep_ref, wts_ref, base_ref, label, label_in, index_v, index_s, part, part_x, part_y, whole,
-    in_sem, index_sem, answered, name_sem, z_send, z_recv, halo_send, halo_recv, disp_send, disp_recv,
+    in_sem, answered, name_sem, z_send, z_recv, halo_send, halo_recv, disp_send, disp_recv,
 ):
     fl = nf * nl
     here, lev, fld = lax.axis_index("horiz"), lax.axis_index("lev"), lax.axis_index("fld")
@@ -52,7 +52,7 @@
         (dep_hbm, dep_ref), (wts_hbm, wts_ref), (base_hbm, base_ref),
         (adj_hbm, adj), (interp_hbm, interp), (traj_hbm, traj),
     ]
-    loads = [pltpu.make_async_copy(src, dst, in_sem.at[i]) for i, (src, dst) in enumerate(pairs)]
+    loads = [pltpu.make_async_copy(src, dst, in_sem.at[i % 5]) for i, (src, dst) in enumerate(pairs)]
     for load in loads[:5]:
         load.start()
 
@@ -88,7 +88,7 @@
     index_v[...] = jnp.broadcast_to(source, index_v.shape)
     for r in range(ROLES):
         label[r] = jnp.broadcast_to(target, label.shape[1:])
-    index_copy = pltpu.make_async_copy(index_v, index_s, index_sem)
+    index_copy = pltpu.make_async_copy(index_v, index_s, in_sem.at[0])
     index_copy.start()
     own_hit = jnp.where((lane_role == ROLES) & (lax.rem(by_lane, tiles) == row), 1.0, 0.0).astype(BF16)
 
@@ -453,9 +453,9 @@
             pltpu.VMEM((fl, tiles, cols), BF16),
             pltpu.VMEM((tiles, cols, cols), BF16),
             pltpu.VMEM((2, fl, tiles, cols), BF16),
-            pltpu.VMEM((fl * tiles, cols), F32),
-            pltpu.VMEM((fl * SLOTS, cols), F32),
-            pltpu.VMEM((fl * tiles, cols), F32),
+            pltpu.VMEM((fl * tiles + tiles, cols), F32),
+            pltpu.VMEM((fl * SLOTS + SLOTS, cols), F32),
+            pltpu.VMEM((fl * tiles + tiles, cols), F32),
             pltpu.VMEM((nf, nl, SLOTS, cols), F32),
             pltpu.VMEM((nf, nl, SLOTS, cols), F32),
             halo_slots, halo_slots, halo_own, halo_own,
@@ -470,7 +470,7 @@
             pltpu.VMEM((flds - 1, 2, span, cols), F32),
             pltpu.VMEM((levs - 1, 2, short, cols), F32),
             pltpu.VMEM((2, tiles, cols), F32),
-            dma((6,)), dma, pltpu.SemaphoreType.REGULAR, dma((2,)), dma, dma((2 + 2 * nf,)),
+            dma((5,)), pltpu.SemaphoreType.REGULAR, dma((2,)), dma, dma((2 + 2 * nf,)),
             dma((2,)), dma((2,)), dma((4,)), dma((4,)),
         ],
         compiler_params=pltpu.CompilerParams(

time: 41.2 us -> 41.2 us (level)
  no operation moved by 1% of the time
where the time goes in v5:
time: 41.2 us; the launch traced here: 41.1 us
  Pallas kernels  40.4 us (98%)
  between operations  0.64 us (2%)
    pallas_call x1, Pallas kernels, shards(): pl.pallas_call(functools.partial(kernel, blocks, levs, flds, nf, nl, tile...  39.1 us
    pallas_call x1, Pallas kernels, shards(): pl.pallas_call(deliver, out_shape=(pltpu.HBM(field.shape, F32), pltpu.HBM...  1.36 us

profile of v5, /device:TPU:1, one launch (start us, length us, event | category | flops | bytes accessed | tf_op | source)
XLA Modules:
  0.0 41.1 jit_solution(6217294803863765231)
XLA Ops:
  0.6 39.1 %shard_map.77 = (f32[2,16,128,128]{3,2,1,0:T(8,128)S(1)}, f32[2,128,128]{2,1,0:T(8,128)S(1)}) custom-call(bf16[32,128,128]{2,1,0:T(8,128)(2,1)} %bitcast.5, bf16[128,128,128]{2,1,0:T(8,128)(2,1)} %interp_hbm.1, bf16[2,32,128,128]{3,2,1,0:T(8,128)(2,1)} %bitcast.4, s32[1,128]{1,0:T(1,128)} %bitcast.7, f32[4,16]{1,0:T(4,128)} %bitcast.6, s32[16]{0:T(128)} %base_hbm.1), custom_call_target="tpu_custom_call" | custom-call | tf_op jit(solution)/shard_map/pallas_call | solution.py:444
  39.7 1.4 %shard_map.78 = (f32[2,16,128,128]{3,2,1,0:T(8,128)}, f32[2,128,128]{2,1,0:T(8,128)}) custom-call(f32[2,16,128,128]{3,2,1,0:T(8,128)S(1)} %get-tuple-element.4.field_ref, f32[2,128,128]{2,1,0:T(8,128)S(1)} %get-tuple-element.5.disp_ref), custom_call_target="tpu_custom_call" | custom-call | tf_op jit(solution)/shard_map/pallas_call | solution.py:486

commit v6 on v5

--- a/solution.py
+++ b/solution.py
@@ -128,7 +128,7 @@
         for b in range(fl // 8):
             dest[pl.ds(s + b * 8 * extent, 8, stride=extent), :] = value[b * 8 : b * 8 + 8]
 
-    def work(g):
+    def work(g, send=None):
         at = pl.multiple_of(g * GROUP, GROUP)
         for i in range(GROUP):
             horizontal(index_s[0, at + i], at + i, h_slot, SLOTS)
@@ -146,12 +146,14 @@
                     slot_edge[1, f, e - nl - 2, pl.ds(at, GROUP), :] = value
 
             vertical(values, emit)
-
-    def inner(g):
+            if send is not None:
+                send(g, f)
+
+    def inner(g, f):
         role = g // GROUPS
         partner = jnp.where(role == 0, pole, jnp.where(role == 1, across, mate))
         at = pl.multiple_of(g * GROUP, GROUP)
-        piece = (slice(None), pl.ds(2, nl - 4), pl.ds(at, GROUP), slice(None))
+        piece = (f, pl.ds(2, nl - 4), pl.ds(at, GROUP), slice(None))
         return pltpu.make_async_remote_copy(
             src_ref=snd.at[piece], dst_ref=rcv.at[piece],
             send_sem=z_send, recv_sem=z_recv.at[jnp.where(role == 0, 0, 1)],
@@ -160,7 +162,8 @@
 
     work(0)
     pl.semaphore_wait(barrier, ROLES + lev + fld)
-    inner(0).start()
+    for f in range(nf):
+        inner(0, f).start()
     for axis, me, size in (("lev", lev, levs), ("fld", fld, flds)):
         for d in range(1, size):
 
@@ -170,8 +173,7 @@
 
 
     def step(g, carry):
-        work(g)
-        inner(g).start()
+        work(g, lambda g, f: inner(g, f).start())
         return carry
 
     def both(g, carry):

time: 41.2 us -> 41.2 us (level)
  no operation moved by 1% of the time
where the time goes in v6:
time: 41.2 us; the launch traced here: 41.1 us
  Pallas kernels  40.4 us (98%)
  between operations  0.64 us (2%)
    pallas_call x1, Pallas kernels, shards(): pl.pallas_call(functools.partial(kernel, blocks, levs, flds, nf, nl, tile...  39.1 us
    pallas_call x1, Pallas kernels, shards(): pl.pallas_call(deliver, out_shape=(pltpu.HBM(field.shape, F32), pltpu.HBM...  1.36 us

profile of v6, /device:TPU:1, one launch (start us, length us, event | category | flops | bytes accessed | tf_op | source)
XLA Modules:
  0.0 41.1 jit_solution(9356368547559396909)
XLA Ops:
  0.6 39.1 %shard_map.77 = (f32[2,16,128,128]{3,2,1,0:T(8,128)S(1)}, f32[2,128,128]{2,1,0:T(8,128)S(1)}) custom-call(bf16[32,128,128]{2,1,0:T(8,128)(2,1)} %bitcast.5, bf16[128,128,128]{2,1,0:T(8,128)(2,1)} %interp_hbm.1, bf16[2,32,128,128]{3,2,1,0:T(8,128)(2,1)} %bitcast.4, s32[1,128]{1,0:T(1,128)} %bitcast.7, f32[4,16]{1,0:T(4,128)} %bitcast.6, s32[16]{0:T(128)} %base_hbm.1), custom_call_target="tpu_custom_call" | custom-call | tf_op jit(solution)/shard_map/pallas_call | solution.py:446
  39.7 1.4 %shard_map.78 = (f32[2,16,128,128]{3,2,1,0:T(8,128)}, f32[2,128,128]{2,1,0:T(8,128)}) custom-call(f32[2,16,128,128]{3,2,1,0:T(8,128)S(1)} %get-tuple-element.4.field_ref, f32[2,128,128]{2,1,0:T(8,128)S(1)} %get-tuple-element.5.disp_ref), custom_call_target="tpu_custom_call" | custom-call | tf_op jit(solution)/shard_map/pallas_call | solution.py:488
